TPU v7x, 32 devices: a whole 2x2x4 slice. The times are simulated.
32 devices in a mesh: runs: 2 (over x), tile: 16 (over z, y, core).
Axes of the slice: x: 2, y: 2, z: 4, core: 2. Of those that a mesh axis runs over, the one named last changes fastest.
Arguments:
- image_stack: bfloat16 [64, 144, 256], P(('runs', 'tile')), parts along dimension 0, may hold values from -6 to 6
- tissue_rows: int32 [64], P(('runs', 'tile')), parts along dimension 0, may hold values from 0 to 12, as said below
- filters: bfloat16 [256, 7744], replicated, may hold values from -24 to 24
- codes_start: bfloat16 [64, 9216], P(('runs', 'tile')), parts along dimension 0, may hold values from -4 to 4
- duals_start: bfloat16 [64, 9216], P(('runs', 'tile')), parts along dimension 0, may hold values from -2 to 2
Outputs:
- sparse_codes: float32 [64, 9216], P(('runs', 'tile')), parts along dimension 0
- dual_state: float32 [64, 9216], P(('runs', 'tile')), parts along dimension 0
- new_filters: bfloat16 [512, 7744], P('runs'), parts along dimension 0
There are 2 independent parts, one for each index of `runs`. A program takes and returns all parts, laid end to end along the dimension named above; an argument that names none is the same for every part. Nothing has to cross between parts.
Inputs may be any that keep to these rules, and one draw needn't show every extreme that they name: `tissue_rows`: each device holds 2 slots; a slot is occupied when its row count is positive, and a device's occupied slots come first. Devices 2j and 2j + 1 of the tile axis hold exactly 2 occupied slots together, and some pair has all of them on one device. The first slot of a device with an occupied slot has all 12 rows.
All inputs are finite; a program needn't handle non-finite values.
Results may differ from a plain program's by a relative error of at most 0.03.
Values may be sent and summed in bfloat16 or wider, within the bound.
A program may use at most 128 MiB of HBM per device.

v0:
```python
import math

import jax
import jax.numpy as jnp
from jax import lax
from jax.sharding import PartitionSpec as P

M = 64
C = 256
K = 11
SIDE = 12
ITERS = 2


PENALTY = 10.0
SPARSITY = 2.0
EPSILON = 1e-05
RELAX = 1.8


def patches_of(code_maps):
    number = code_maps.shape[0]
    margin = (K - 1) // 2
    padded = jnp.pad(code_maps, ((0, 0), (margin, margin), (margin, margin), (0, 0)))
    columns = [
        padded[:, row_off : row_off + SIDE, col_off : col_off + SIDE, :]
        for row_off in range(K)
        for col_off in range(K)
    ]
    return jnp.stack(columns, axis=3).reshape(number * SIDE * SIDE, K * K * M)


def fold_back(correlation):
    number = correlation.shape[0] // (SIDE * SIDE)
    margin = (K - 1) // 2
    shaped = correlation.reshape(number, SIDE, SIDE, K * K, M)
    summed = jnp.zeros((number, SIDE, SIDE, M), jnp.float32)
    for row_off in range(K):
        for col_off in range(K):
            top = 2 * margin - row_off
            left = 2 * margin - col_off
            piece = shaped[:, :, :, row_off * K + col_off, :].astype(jnp.float32)
            padded = jnp.pad(piece, ((0, 0), (margin, margin), (margin, margin), (0, 0)))
            summed = summed + padded[:, top : top + SIDE, left : left + SIDE, :]
    return summed.reshape(number, SIDE * SIDE, M)


def normalized(moved, squares):
    rows_here = moved.shape[0]
    norms = jnp.sqrt(squares / (C * K * K) + EPSILON)
    return (
        (moved.reshape(rows_here, K * K, M) / norms)
        .reshape(rows_here, K * K * M)
        .astype(jnp.bfloat16)
    )


def admm_update(codes_now, duals_now, gradient):
    primal = codes_now - duals_now - gradient / PENALTY
    relaxed = RELAX * primal + (1.0 - RELAX) * codes_now
    merged = relaxed + duals_now
    shrunk = jnp.sign(merged) * jnp.maximum(jnp.abs(merged) - SPARSITY / PENALTY, 0.0)
    return (shrunk, duals_now + relaxed - shrunk)


def residual_pass(current, images, tissue, codes_now):
    factor = 1.0 / math.sqrt(K * K * M)
    number = images.shape[0]
    patches = patches_of(codes_now.astype(jnp.bfloat16).reshape(number, SIDE, SIDE, M))
    rebuilt = jnp.dot(patches, current.T, preferred_element_type=jnp.float32) * factor
    flat_images = images.reshape(number * SIDE * SIDE, C).astype(jnp.float32)
    residual = (tissue * (rebuilt - flat_images)).astype(jnp.bfloat16)
    correlation = (jnp.dot(residual, current, preferred_element_type=jnp.float32) * factor).astype(
        jnp.bfloat16
    )
    return (patches, residual, fold_back(correlation))


def term_maker(residual, patches):
    factor = 1.0 / math.sqrt(K * K * M)
    return (
        lax.dot_general(
            residual, patches, (((0,), (0,)), ((), ())), preferred_element_type=jnp.float32
        )
        * factor
    )


def own_rows(current, row_share):
    return lax.dynamic_slice_in_dim(
        current, lax.axis_index("tile") * row_share, row_share, 0
    ).astype(jnp.float32)


def dictionary_step(filters, residual, patches, stride, row_share):
    share = lax.psum_scatter(term_maker(residual, patches), "tile", scatter_dimension=0, tiled=True)
    moved = own_rows(filters, row_share) - stride * share
    squares = jnp.sum((moved * moved).reshape(moved.shape[0], K * K, M), axis=(0, 1))
    totals = lax.psum(squares, "tile")
    return lax.all_gather(normalized(moved, totals), "tile", axis=0, tiled=True)


def local(image_stack, tissue_rows, filters, codes_start, duals_start):
    slot_count = image_stack.shape[0]
    pixels = image_stack.shape[1]
    groups = lax.axis_size("tile")
    row_share = C // groups
    stride = 0.5 * math.sqrt(K * K * M / (pixels * slot_count * groups))
    work_codes = codes_start.astype(jnp.float32).reshape(slot_count, pixels, M)
    work_duals = duals_start.astype(jnp.float32).reshape(slot_count, pixels, M)
    tissue = (
        (jnp.arange(pixels)[None, :] // SIDE < tissue_rows[:, None])
        .astype(jnp.float32)
        .reshape(-1, 1)
    )
    new_filters = filters
    for iteration in range(ITERS):
        patches, residual, gradient = residual_pass(filters, image_stack, tissue, work_codes)
        if iteration == ITERS - 1:
            new_filters = dictionary_step(filters, residual, patches, stride, row_share)
        work_codes, work_duals = admm_update(work_codes, work_duals, gradient)
    return (
        work_codes.reshape(slot_count, pixels * M),
        work_duals.reshape(slot_count, pixels * M),
        new_filters,
    )


def solution(mesh):
    return jax.shard_map(
        local,
        mesh=mesh,
        in_specs=(
            P(("runs", "tile"), None, None),
            P(("runs", "tile")),
            P(),
            P(("runs", "tile"), None),
            P(("runs", "tile"), None),
        ),
        out_specs=(P(("runs", "tile"), None), P(("runs", "tile"), None), P("runs", None)),
        check_vma=False,
    )
```

profile of v0, /device:TPU:0, one launch (start us, length us, event | category | flops | bytes accessed | tf_op | source)
XLA Modules:
  0.0 531.6 jit_solution(16657176841145175480)
XLA Ops:
  89.4 13.8 %copy.987 = bf16[2,12,12,121,64]{4,3,2,1,0:T(8,128)(2,1)} copy(bf16[2,12,12,121,64]{4,2,1,0,3:T(8,128)(2,1)} %constant_dynamic-update-slice_fusion) | data formatting | bytes 8921088 | tf_op jit(solution)/shard_map/stack | solution.py:30
  103.2 13.1 %reshape.611 = bf16[288,7744]{1,0:T(8,128)(2,1)} reshape(bf16[2,12,12,121,64]{4,3,2,1,0:T(8,128)(2,1)} %copy.987) | data formatting | bytes 8921088 | tf_op jit(solution)/shard_map/reshape | solution.py:30
  116.5 11.7 %fusion = bf16[288,7744]{1,0:T(8,128)(2,1)} fusion(bf16[256,7744]{0,1:T(8,128)(2,1)} %param.7, bf16[288,7744]{1,0:T(8,128)(2,1)} %reshape.611, bf16[288,256]{1,0:T(8,128)(2,1)S(1)} %bitcast.1710, f32[288]{0:T(512)S(1)} %reshape.616), kind=kOutput, calls=%fused_computation.3 | convolution fusion | flops 2288627712 | bytes 13034624 | tf_op jit(solution)/shard_map/dot_general | solution.py:73
  128.2 13.5 %reshape.612 = bf16[2,12,12,121,64]{4,3,2,1,0:T(8,128)(2,1)} reshape(bf16[288,7744]{1,0:T(8,128)(2,1)} %fusion) | data formatting | bytes 8921088 | tf_op jit(solution)/shard_map/reshape | solution.py:36
  141.7 8.3 %fusion.311 = (bf16[2,12,12,1,64]{4,3,2,1,0:T(2,128)(2,1)}, bf16[2,12,12,1,64]{4,3,2,1,0:T(2,128)(2,1)S(1)}, bf16[2,12,12,1,64]{4,3,2,1,0:T(2,128)(2,1)S(1)}, bf...) fusion(bf16[2,12,12,121,64]{4,3,2,1,0:T(8,128)(2,1)} %reshape.612), kind=kLoop, calls=%fused_computation.1297 | loop fusion | bytes 1400832 | tf_op jit(solution)/shard_map/slice | solution.py:42
  150.0 8.4 %fusion.312 = (bf16[2,12,12,1,64]{4,3,2,1,0:T(2,128)(2,1)}, bf16[2,12,12,1,64]{4,3,2,1,0:T(2,128)(2,1)}, bf16[2,12,12,1,64]{4,3,2,1,0:T(2,128)(2,1)}, bf16[2,12,...) fusion(bf16[2,12,12,121,64]{4,3,2,1,0:T(8,128)(2,1)} %reshape.612), kind=kLoop, calls=%fused_computation.1298 | loop fusion | bytes 1400832 | tf_op jit(solution)/shard_map/slice | solution.py:42
  158.5 4.0 fusion.314
  162.5 4.4 fusion.315
  168.5 4.1 fusion.313
  172.6 3.9 fusion.310
  210.2 4.2 multiply_convert_fusion
  294.8 13.8 %copy.1110 = bf16[2,12,12,121,64]{4,3,2,1,0:T(8,128)(2,1)} copy(bf16[2,12,12,121,64]{4,2,1,0,3:T(8,128)(2,1)} %constant_dynamic-update-slice_fusion.121) | data formatting | bytes 8921088 | tf_op jit(solution)/shard_map/stack | solution.py:30
  308.6 13.1 %reshape.614 = bf16[288,7744]{1,0:T(8,128)(2,1)} reshape(bf16[2,12,12,121,64]{4,3,2,1,0:T(8,128)(2,1)} %copy.1110) | data formatting | bytes 8921088 | tf_op jit(solution)/shard_map/reshape | solution.py:30
  321.8 5.0 fusion.6
  326.8 5.5 %convolution_multiply_fusion.2 = f32[256,7744]{1,0:T(8,128)} fusion(bf16[288,256]{1,0:T(8,128)(2,1)S(1)} %fusion.6, bf16[288,7744]{1,0:T(8,128)(2,1)S(1)} %copy-done.1), kind=kOutput, calls=%fused_computation.2 | convolution fusion | flops 1143881728 | bytes 12537856 | tf_op jit(solution)/shard_map/dot_general | solution.py:82
  336.1 5.7 %fusion.1 = bf16[288,7744]{1,0:T(8,128)(2,1)} fusion(bf16[288,256]{1,0:T(8,128)(2,1)S(1)} %fusion.6, bf16[256,7744]{0,1:T(8,128)(2,1)} %param.7), kind=kOutput, calls=%fused_computation.4 | convolution fusion | flops 1146359808 | bytes 8572928 | tf_op jit(solution)/shard_map/dot_general | solution.py:73
  341.8 13.9 %reshape.615 = bf16[2,12,12,121,64]{4,3,2,1,0:T(8,128)(2,1)} reshape(bf16[288,7744]{1,0:T(8,128)(2,1)} %fusion.1) | data formatting | bytes 8921088 | tf_op jit(solution)/shard_map/reshape | solution.py:36
  355.6 80.3 %reduce-scatter.2.cloned.1.call-done = f32[16,7744]{1,0:T(8,128)} async-done(((f32[256,7744]{1,0:T(8,128)}), f32[16,7744]{1,0:T(8,128)}) %reduce-scatter.2.cloned.1.call-update) | async-done | bytes 495632 | tf_op jit(solution)/shard_map/reduce_scatter | solution.py:96
  437.2 32.2 %psum.7 = f32[64]{0:T(128)S(1)} all-reduce(f32[64]{0:T(128)S(1)} %reduce_sum.18), channel_id=1, replica_groups=mesh['runs'=2,'tile'=16] {'tile'}, use_global_device_ids=true, to_apply=%region_3.4 | all-reduce | flops 64 | bytes 512 | tf_op jit(solution)/shard_map/psum | solution.py:99
  471.4 7.5 %fusion.304 = (bf16[2,12,12,1,64]{4,3,2,1,0:T(2,128)(2,1)S(1)}, bf16[2,12,12,1,64]{4,3,2,1,0:T(2,128)(2,1)S(1)}, bf16[2,12,12,1,64]{4,3,2,1,0:T(2,128)(2,1)S(1)}...) fusion(bf16[2,12,12,121,64]{4,3,2,1,0:T(8,128)(2,1)} %reshape.615), kind=kLoop, calls=%fused_computation.1290 | loop fusion | bytes 1400832 | tf_op jit(solution)/shard_map/slice | solution.py:42
  478.9 7.1 %fusion.303 = (bf16[2,12,12,1,64]{4,3,2,1,0:T(2,128)(2,1)S(1)}, bf16[2,12,12,1,64]{4,3,2,1,0:T(2,128)(2,1)S(1)}, bf16[2,12,12,1,64]{4,3,2,1,0:T(2,128)(2,1)S(1)}...) fusion(bf16[2,12,12,121,64]{4,3,2,1,0:T(8,128)(2,1)} %reshape.615), kind=kLoop, calls=%fused_computation.1289 | loop fusion | bytes 1400832 | tf_op jit(solution)/shard_map/slice | solution.py:42
  500.9 4.2 add_multiply_fusion
  506.4 11.6 %all-gather.2.cloned.1.call-done = bf16[256,7744]{1,0:T(8,128)(2,1)} async-done(((bf16[16,7744]{1,0:T(8,128)(2,1)}), bf16[256,7744]{1,0:T(8,128)(2,1)}) %all-gather.2.cloned.1.call-update) | async-done | bytes 3964944 | tf_op jit(solution)/shard_map/all_gather | solution.py:100
  518.0 6.3 %copy.1233 = bf16[256,7744]{0,1:T(8,128)(2,1)} copy(bf16[256,7744]{1,0:T(8,128)(2,1)} %all-gather.2.cloned.1.call-done) | data formatting | bytes 7929856
  (560 shorter events, 219.3 us)
Async XLA Ops:
  7.2 428.8 %reduce-scatter.2.cloned.1.call-start = ((), (), s32[]{:S(2)}) async-start(), calls=%async_computation.1 | async-start | bytes 8495104 | tf_op jit(solution)/shard_map/reduce_scatter | solution.py:96
  178.0 30.6 %copy-start.39 = (bf16[2,12,12,1,64]{4,3,2,1,0:T(2,128)(2,1)S(1)}, bf16[2,12,12,1,64]{4,3,2,1,0:T(2,128)(2,1)}, u32[]{:S(2)}) copy-start(bf16[2,12,12,1,64]{4,3,2,1,0:T(2,128)(2,1)} %get-tuple-element.200) | copy-start | bytes 110596
  178.0 30.6 %copy-start.37 = (bf16[2,12,12,1,64]{4,3,2,1,0:T(2,128)(2,1)S(1)}, bf16[2,12,12,1,64]{4,3,2,1,0:T(2,128)(2,1)}, u32[]{:S(2)}) copy-start(bf16[2,12,12,1,64]{4,3,2,1,0:T(2,128)(2,1)} %get-tuple-element.198) | copy-start | bytes 110596
  178.0 30.6 %copy-start.38 = (bf16[2,12,12,1,64]{4,3,2,1,0:T(2,128)(2,1)S(1)}, bf16[2,12,12,1,64]{4,3,2,1,0:T(2,128)(2,1)}, u32[]{:S(2)}) copy-start(bf16[2,12,12,1,64]{4,3,2,1,0:T(2,128)(2,1)} %get-tuple-element.199) | copy-start | bytes 110596
  178.0 30.7 %copy-start.35 = (bf16[2,12,12,1,64]{4,3,2,1,0:T(2,128)(2,1)S(1)}, bf16[2,12,12,1,64]{4,3,2,1,0:T(2,128)(2,1)}, u32[]{:S(2)}) copy-start(bf16[2,12,12,1,64]{4,3,2,1,0:T(2,128)(2,1)} %get-tuple-element.195) | copy-start | bytes 110596
  178.1 30.7 %copy-start.36 = (bf16[2,12,12,1,64]{4,3,2,1,0:T(2,128)(2,1)S(1)}, bf16[2,12,12,1,64]{4,3,2,1,0:T(2,128)(2,1)}, u32[]{:S(2)}) copy-start(bf16[2,12,12,1,64]{4,3,2,1,0:T(2,128)(2,1)} %get-tuple-element.196) | copy-start | bytes 110596
  178.1 30.7 %copy-start.33 = (bf16[2,12,12,1,64]{4,3,2,1,0:T(2,128)(2,1)S(1)}, bf16[2,12,12,1,64]{4,3,2,1,0:T(2,128)(2,1)}, u32[]{:S(2)}) copy-start(bf16[2,12,12,1,64]{4,3,2,1,0:T(2,128)(2,1)} %get-tuple-element.193) | copy-start | bytes 110596
  178.1 30.7 %copy-start.34 = (bf16[2,12,12,1,64]{4,3,2,1,0:T(2,128)(2,1)S(1)}, bf16[2,12,12,1,64]{4,3,2,1,0:T(2,128)(2,1)}, u32[]{:S(2)}) copy-start(bf16[2,12,12,1,64]{4,3,2,1,0:T(2,128)(2,1)} %get-tuple-element.194) | copy-start | bytes 110596
  178.1 30.7 %copy-start.29 = (bf16[2,12,12,1,64]{4,3,2,1,0:T(2,128)(2,1)S(1)}, bf16[2,12,12,1,64]{4,3,2,1,0:T(2,128)(2,1)}, u32[]{:S(2)}) copy-start(bf16[2,12,12,1,64]{4,3,2,1,0:T(2,128)(2,1)} %get-tuple-element.191) | copy-start | bytes 110596
  178.1 30.7 %copy-start.30 = (bf16[2,12,12,1,64]{4,3,2,1,0:T(2,128)(2,1)S(1)}, bf16[2,12,12,1,64]{4,3,2,1,0:T(2,128)(2,1)}, u32[]{:S(2)}) copy-start(bf16[2,12,12,1,64]{4,3,2,1,0:T(2,128)(2,1)} %get-tuple-element.192) | copy-start | bytes 110596
  178.1 30.8 %copy-start.25 = (bf16[2,12,12,1,64]{4,3,2,1,0:T(2,128)(2,1)S(1)}, bf16[2,12,12,1,64]{4,3,2,1,0:T(2,128)(2,1)}, u32[]{:S(2)}) copy-start(bf16[2,12,12,1,64]{4,3,2,1,0:T(2,128)(2,1)} %get-tuple-element.189) | copy-start | bytes 110596
  178.1 30.8 %copy-start.26 = (bf16[2,12,12,1,64]{4,3,2,1,0:T(2,128)(2,1)S(1)}, bf16[2,12,12,1,64]{4,3,2,1,0:T(2,128)(2,1)}, u32[]{:S(2)}) copy-start(bf16[2,12,12,1,64]{4,3,2,1,0:T(2,128)(2,1)} %get-tuple-element.190) | copy-start | bytes 110596
  178.1 30.8 %copy-start.21 = (bf16[2,12,12,1,64]{4,3,2,1,0:T(2,128)(2,1)S(1)}, bf16[2,12,12,1,64]{4,3,2,1,0:T(2,128)(2,1)}, u32[]{:S(2)}) copy-start(bf16[2,12,12,1,64]{4,3,2,1,0:T(2,128)(2,1)} %get-tuple-element.187) | copy-start | bytes 110596
  178.1 30.8 %copy-start.22 = (bf16[2,12,12,1,64]{4,3,2,1,0:T(2,128)(2,1)S(1)}, bf16[2,12,12,1,64]{4,3,2,1,0:T(2,128)(2,1)}, u32[]{:S(2)}) copy-start(bf16[2,12,12,1,64]{4,3,2,1,0:T(2,128)(2,1)} %get-tuple-element.188) | copy-start | bytes 110596
  178.1 30.9 %copy-start.17 = (bf16[2,12,12,1,64]{4,3,2,1,0:T(2,128)(2,1)S(1)}, bf16[2,12,12,1,64]{4,3,2,1,0:T(2,128)(2,1)}, u32[]{:S(2)}) copy-start(bf16[2,12,12,1,64]{4,3,2,1,0:T(2,128)(2,1)} %get-tuple-element.185) | copy-start | bytes 110596
  178.2 30.9 %copy-start.18 = (bf16[2,12,12,1,64]{4,3,2,1,0:T(2,128)(2,1)S(1)}, bf16[2,12,12,1,64]{4,3,2,1,0:T(2,128)(2,1)}, u32[]{:S(2)}) copy-start(bf16[2,12,12,1,64]{4,3,2,1,0:T(2,128)(2,1)} %get-tuple-element.186) | copy-start | bytes 110596
  178.2 30.9 %copy-start.13 = (bf16[2,12,12,1,64]{4,3,2,1,0:T(2,128)(2,1)S(1)}, bf16[2,12,12,1,64]{4,3,2,1,0:T(2,128)(2,1)}, u32[]{:S(2)}) copy-start(bf16[2,12,12,1,64]{4,3,2,1,0:T(2,128)(2,1)} %get-tuple-element.183) | copy-start | bytes 110596
  178.2 30.9 %copy-start.14 = (bf16[2,12,12,1,64]{4,3,2,1,0:T(2,128)(2,1)S(1)}, bf16[2,12,12,1,64]{4,3,2,1,0:T(2,128)(2,1)}, u32[]{:S(2)}) copy-start(bf16[2,12,12,1,64]{4,3,2,1,0:T(2,128)(2,1)} %get-tuple-element.184) | copy-start | bytes 110596
  178.2 31.0 %copy-start.9 = (bf16[2,12,12,1,64]{4,3,2,1,0:T(2,128)(2,1)S(1)}, bf16[2,12,12,1,64]{4,3,2,1,0:T(2,128)(2,1)}, u32[]{:S(2)}) copy-start(bf16[2,12,12,1,64]{4,3,2,1,0:T(2,128)(2,1)} %get-tuple-element.181) | copy-start | bytes 110596
  178.2 31.0 %copy-start.10 = (bf16[2,12,12,1,64]{4,3,2,1,0:T(2,128)(2,1)S(1)}, bf16[2,12,12,1,64]{4,3,2,1,0:T(2,128)(2,1)}, u32[]{:S(2)}) copy-start(bf16[2,12,12,1,64]{4,3,2,1,0:T(2,128)(2,1)} %get-tuple-element.182) | copy-start | bytes 110596
  178.2 31.0 %copy-start.5 = (bf16[2,12,12,1,64]{4,3,2,1,0:T(2,128)(2,1)S(1)}, bf16[2,12,12,1,64]{4,3,2,1,0:T(2,128)(2,1)}, u32[]{:S(2)}) copy-start(bf16[2,12,12,1,64]{4,3,2,1,0:T(2,128)(2,1)} %get-tuple-element.179) | copy-start | bytes 110596
  178.2 31.0 %copy-start.6 = (bf16[2,12,12,1,64]{4,3,2,1,0:T(2,128)(2,1)S(1)}, bf16[2,12,12,1,64]{4,3,2,1,0:T(2,128)(2,1)}, u32[]{:S(2)}) copy-start(bf16[2,12,12,1,64]{4,3,2,1,0:T(2,128)(2,1)} %get-tuple-element.180) | copy-start | bytes 110596
  332.3 185.8 %all-gather.2.cloned.1.call-start = ((), (), s32[]{:S(2)}) async-start(), calls=%async_computation.2 | async-start | bytes 4247552 | tf_op jit(solution)/shard_map/all_gather | solution.py:100
  355.6 131.3 %slice-start = ((s8[9437184]{0:T(1024)(128)(4,1)}), s8[1048576]{0:T(1024)(128)(4,1)S(1)}, s32[]{:S(2)}) async-start(s8[9437184]{0:T(1024)(128)(4,1)} %bitcast.1586), calls=%async_computation.3 | async-start | bytes 2097152
  (31 other events, 616.8 us)
Sparse Core Ops, SparseCore 0:
  332.4 103.5 reduce-scatter.1
  471.5 46.4 all-gather.1
where the time goes:
time: 542 us; the launch traced here: 532 us
  local copies, waits for them, and re-layouts  350 us (65%)
  waiting for transfers between devices  91.9 us (17%)
  blocking collectives  32.2 us (6%)
  matrix products  27.8 us (5%)
  between operations  16.8 us (3%)
  other arithmetic  12.6 us (2%)
    unnamed x469, local copies, waits for them, and re-layouts  172 us
    reduce_scatter x1, waiting for transfers between devices, dictionary_step(): lax.psum_scatter(term_maker(residual, patches), 'tile', scatter_dimension...  80.3 us
    slice x15, local copies, waits for them, and re-layouts, fold_back(): piece = shaped[:, :, :, row_off * K + col_off, :].astype(jnp.float32)  59.8 us
    psum x1, blocking collectives, dictionary_step(): totals = lax.psum(squares, 'tile')  32.2 us
    convert_element_type x60, local copies, waits for them, and re-layouts, fold_back(): piece = shaped[:, :, :, row_off * K + col_off, :].astype(jnp.float32)  31.7 us
    another operation x4, local copies, waits for them, and re-layouts, patches_of(): return jnp.stack(columns, axis=3).reshape(number * SIDE * SIDE, K * K * M)  29 us
    reshape x2, local copies, waits for them, and re-layouts, fold_back(): shaped = correlation.reshape(number, SIDE, SIDE, K * K, M)  27.4 us
    reshape x2, local copies, waits for them, and re-layouts, patches_of(): return jnp.stack(columns, axis=3).reshape(number * SIDE * SIDE, K * K * M)  26.2 us
  transfers between devices with their start and end apart: 2, of which 2 were waited for; matrix products, arithmetic and copies ran while one was open for 11% of the time, Pallas kernels for 0%

commit v1 on v0

v1 whole, which is shorter than its diff:
```python
import math

import jax
import jax.numpy as jnp
from jax import lax
from jax.experimental import pallas as pl
from jax.experimental.pallas import tpu as pltpu
from jax.sharding import PartitionSpec as P

M = 64
C = 256
K = 11
SIDE = 12
JP = 16
PAIR = 2 * K * M
LAST = K * M
COLS = K * K * M
BLOCKS = PAIR // 128
FACTOR = 1.0 / math.sqrt(K * K * M)

PENALTY = 10.0
SPARSITY = 2.0
EPSILON = 1e-05
RELAX = 1.8

F32 = jnp.float32
BF16 = jnp.bfloat16


def put_codes(dpad, codes):
    both = jnp.concatenate([codes, codes], axis=-1)
    dpad[5 : 5 + SIDE, :, 6 : 6 + SIDE, 0:M] = both[..., 0:M]
    dpad[5 : 5 + SIDE, :, 5 : 5 + SIDE, M : 2 * M] = both[..., M : 2 * M]


def build_taps(dpad, taps):
    slots = dpad.shape[1]
    rows = 22 * slots * JP
    for q in range(BLOCKS):
        if q < 5:
            block = dpad[0:22, :, 2 * q + 1 : 2 * q + 1 + JP, :]
        elif q > 5:
            start = 2 * (q - 6) + 2
            block = dpad[1:23, :, start : start + JP, :]
        else:
            low = dpad[0:22, :, 11 : 11 + JP, :]
            high = dpad[1:23, :, 0:JP, :]
            lane = lax.broadcasted_iota(jnp.int32, low.shape, 3)
            block = jnp.where(lane < M, low, high)
        taps[:, q * 128 : (q + 1) * 128] = block.reshape(rows, 128).astype(BF16)


def rebuild(taps, f_ref, slots):
    rows = SIDE * slots * JP
    total = None
    for p in range(6):
        width = PAIR if p < 5 else LAST
        at = p * 2 * slots * JP
        part = lax.dot_general(
            taps[at : at + rows, 0:width],
            f_ref[:, p * PAIR : p * PAIR + width],
            (((1,), (1,)), ((), ())),
            preferred_element_type=F32,
        )
        total = part if total is None else total + part
    return total


def fill_tail(f_ref, ftail):
    ftail[...] = jnp.zeros_like(ftail)
    ftail[:, 0:192] = f_ref[:, COLS - 192 : COLS]


def code_gradient(rpad, f_ref, ftail, zpad, slots):
    rows = 13 * slots * JP
    step = slots * JP
    for n in range(6):
        width = 256 if n < 5 else 128
        acc = None
        for p in range(6):
            at = (10 - 2 * p) * step
            if p < 5:
                piece = f_ref[:, p * PAIR + n * 256 : p * PAIR + n * 256 + width]
            elif n < 2:
                piece = f_ref[:, p * PAIR + n * 256 : p * PAIR + n * 256 + width]
            elif n == 2:
                piece = ftail[...]
            else:
                continue
            part = jnp.dot(rpad[at : at + rows, :], piece, preferred_element_type=F32)
            acc = part if acc is None else acc + part
        for h in range(width // 128):
            zpad[2 * n + h, :, :, 8:24, :] = acc[:, h * 128 : (h + 1) * 128].reshape(
                13, slots, JP, 128
            )
    total = None
    for q in range(BLOCKS):
        if q < 5:
            part = zpad[q, 1:13, :, 12 - 2 * q : 36 - 2 * q, :]
        elif q > 5:
            start = 11 - 2 * (q - 6)
            part = zpad[q, 0:12, :, start : start + 24, :]
        else:
            low = zpad[q, 1:13, :, 2:26, :]
            high = zpad[q, 0:12, :, 13:37, :]
            lane = lax.broadcasted_iota(jnp.int32, low.shape, 3)
            part = jnp.where(lane < M, low, high)
        total = part if total is None else total + part
    zpad[0, 0:12, :, 0:24, :] = total
    low = zpad[0, 0:12, :, 1 : 1 + JP, 0:M]
    high = zpad[0, 0:12, :, 0:JP, M : 2 * M]
    return (low + high) * FACTOR


def admm_update(codes_now, duals_now, gradient):
    primal = codes_now - duals_now - gradient / PENALTY
    relaxed = RELAX * primal + (1.0 - RELAX) * codes_now
    merged = relaxed + duals_now
    level = SPARSITY / PENALTY
    shrunk = jnp.where(
        merged > level, merged - level, jnp.where(merged < -level, merged + level, 0.0)
    )
    return shrunk, duals_now + relaxed - shrunk


def tissue_of(rows_ref, shape):
    row = lax.broadcasted_iota(jnp.int32, shape, 0)
    slot = lax.broadcasted_iota(jnp.int32, shape, 1)
    col = lax.broadcasted_iota(jnp.int32, shape, 2)
    height = jnp.full(shape, 0, jnp.int32)
    for s in range(shape[1]):
        height = jnp.where(slot == s, rows_ref[s], height)
    return (row < height) & (col < SIDE), height > 0


def first_kernel(
    rows_ref, f_ref, img_ref, codes_ref, duals_ref, pay_ref, codes_out, duals_out,
    dpad, taps, rpad, ftail, zpad, stage
):
    slots = img_ref.shape[1]
    rows = SIDE * slots * JP
    lead = 6 * slots * JP
    dpad[...] = jnp.zeros_like(dpad)
    rpad[...] = jnp.zeros_like(rpad)
    zpad[...] = jnp.zeros_like(zpad)
    fill_tail(f_ref, ftail)
    inside, occupied = tissue_of(rows_ref, (SIDE, slots, JP, C))
    codes = codes_ref[...].astype(F32)
    duals = duals_ref[...].astype(F32)
    images = img_ref[...].astype(F32)

    def residual_of(values):
        put_codes(dpad, values[:, :, 0:SIDE, :])
        build_taps(dpad, taps)
        rebuilt = rebuild(taps, f_ref, slots).reshape(SIDE, slots, JP, C) * FACTOR
        return jnp.where(inside, rebuilt - images, 0.0)

    residual = residual_of(codes)
    rpad[lead : lead + rows, :] = residual.reshape(rows, C).astype(BF16)
    gradient = code_gradient(rpad, f_ref, ftail, zpad, slots)
    codes, duals = admm_update(codes, duals, gradient)
    codes_out[...] = codes
    duals_out[...] = duals
    residual = residual_of(codes)
    stage[...] = residual
    held = jnp.where(occupied[..., 0:M], codes, 0.0)
    for k in range(3):
        stage[:, :, SIDE:JP, k * M : (k + 1) * M] = held[:, :, 4 * k : 4 * k + 4, :]
    pay_ref[...] = stage[...].astype(BF16)


def second_kernel(f_ref, pay_ref, codes_ref, duals_ref, codes_out, duals_out, rpad, ftail, zpad):
    slots = pay_ref.shape[1]
    rows = SIDE * slots * JP
    lead = 6 * slots * JP
    rpad[...] = jnp.zeros_like(rpad)
    zpad[...] = jnp.zeros_like(zpad)
    fill_tail(f_ref, ftail)
    payload = pay_ref[...].astype(F32)
    col = lax.broadcasted_iota(jnp.int32, payload.shape, 2)
    residual = jnp.where(col < SIDE, payload, 0.0)
    rpad[lead : lead + rows, :] = residual.reshape(rows, C).astype(BF16)
    gradient = code_gradient(rpad, f_ref, ftail, zpad, slots)
    codes, duals = admm_update(codes_ref[...], duals_ref[...], gradient)
    codes_out[...] = codes
    duals_out[...] = duals


def dictionary_kernel(stride, f_ref, all_ref, new_ref, dpad, taps, stage, total):
    at = pl.program_id(0)
    group = all_ref.shape[0]
    rows = SIDE * group * JP

    @pl.when(at == 0)
    def _():
        dpad[...] = jnp.zeros_like(dpad)
        total[...] = jnp.zeros_like(total)

    for d in range(0, group, 2):
        for k in range(2):
            stage[:, d + k, :, :] = all_ref[d, :, k, :, :].astype(F32) + all_ref[
                d + 1, :, 1 - k, :, :
            ].astype(F32)
    for k in range(3):
        lanes = slice(k * M, (k + 1) * M)
        codes = stage[:, :, SIDE:JP, lanes]
        both = jnp.concatenate([codes, codes], axis=-1)
        dpad[5 : 5 + SIDE, :, 6 + 4 * k : 10 + 4 * k, 0:M] = both[..., 0:M]
        dpad[5 : 5 + SIDE, :, 5 + 4 * k : 9 + 4 * k, M : 2 * M] = both[..., M : 2 * M]
    build_taps(dpad, taps)
    values = stage[...]
    col = lax.broadcasted_iota(jnp.int32, values.shape, 2)
    turned = jnp.where(col < SIDE, values, 0.0).reshape(rows, C).T.astype(BF16)
    for p in range(6):
        width = PAIR if p < 5 else LAST
        start = p * 2 * group * JP
        total[:, p * PAIR : p * PAIR + width] += jnp.dot(
            turned, taps[start : start + rows, 0:width], preferred_element_type=F32
        )

    @pl.when(at == pl.num_programs(0) - 1)
    def _():
        squares = jnp.zeros((C, 128), F32)
        for q in range(COLS // 128 + 1):
            width = min(128, COLS - q * 128)
            lanes = slice(q * 128, q * 128 + width)
            moved = f_ref[:, lanes].astype(F32) - (stride * FACTOR) * total[:, lanes]
            total[:, lanes] = moved
            if width == 128:
                squares = squares + moved * moved
        tail = jnp.sum(moved * moved, axis=0, keepdims=True)
        sums = jnp.sum(squares, axis=0, keepdims=True)
        each = sums[:, 0:M] + sums[:, M : 2 * M] + tail
        inverse = 1.0 / jnp.sqrt(each / (C * K * K) + EPSILON)
        wide = jnp.concatenate([inverse, inverse], axis=-1)
        for q in range(COLS // 128 + 1):
            width = min(128, COLS - q * 128)
            lanes = slice(q * 128, q * 128 + width)
            new_ref[:, lanes] = (total[:, lanes] * wide[:, 0:width]).astype(BF16)


def in_vmem():
    return pl.BlockSpec(memory_space=pltpu.VMEM)


LIMIT = 56 * 1024 * 1024


def cost(flops):
    return pl.CostEstimate(flops=flops, bytes_accessed=8 * 1024 * 1024, transcendentals=0)


def local(image_stack, tissue_rows, filters, codes_start, duals_start):
    slots = image_stack.shape[0]
    groups = lax.axis_size("tile")
    stride = 0.5 * math.sqrt(COLS / (SIDE * SIDE * slots * groups))

    def arranged(array, width):
        shaped = array.reshape(slots, SIDE, SIDE, width).transpose(1, 0, 2, 3)
        return jnp.pad(shaped, ((0, 0), (0, 0), (0, JP - SIDE), (0, 0)))

    state = jax.ShapeDtypeStruct((SIDE, slots, JP, M), F32)
    one_product = 2 * SIDE * SIDE * slots * C * COLS
    back = [
        pltpu.VMEM((23 * slots * JP, C), BF16),
        pltpu.VMEM((C, 256), BF16),
        pltpu.VMEM((BLOCKS, 13, slots, 40, 128), F32),
    ]
    payload, codes_mid, duals_mid = pl.pallas_call(
        first_kernel,
        out_shape=(jax.ShapeDtypeStruct((SIDE, slots, JP, C), BF16), state, state),
        in_specs=[pl.BlockSpec(memory_space=pltpu.SMEM)] + [in_vmem()] * 4,
        out_specs=(in_vmem(),) * 3,
        scratch_shapes=[
            pltpu.VMEM((23, slots, 32, 128), F32),
            pltpu.VMEM((22 * slots * JP, PAIR), BF16),
        ]
        + back
        + [pltpu.VMEM((SIDE, slots, JP, C), F32)],
        compiler_params=pltpu.CompilerParams(vmem_limit_bytes=LIMIT),
        cost_estimate=cost(3 * one_product),
        name="first_pass",
    )(
        tissue_rows,
        filters,
        arranged(image_stack, C),
        arranged(codes_start, M),
        arranged(duals_start, M),
    )
    everyone = lax.all_gather(payload, "tile", axis=0)
    codes, duals = pl.pallas_call(
        second_kernel,
        out_shape=(state, state),
        in_specs=[in_vmem()] * 4,
        out_specs=(in_vmem(),) * 2,
        scratch_shapes=back,
        compiler_params=pltpu.CompilerParams(vmem_limit_bytes=LIMIT),
        cost_estimate=cost(one_product),
        name="second_codes",
    )(filters, payload, codes_mid, duals_mid)
    group = 4 if groups % 4 == 0 else 2
    new_filters = pl.pallas_call(
        lambda *refs: dictionary_kernel(stride, *refs),
        grid=(groups // group,),
        out_shape=jax.ShapeDtypeStruct((C, COLS), BF16),
        in_specs=[
            pl.BlockSpec((C, COLS), lambda g: (0, 0), pipeline_mode=pl.Buffered(1)),
            pl.BlockSpec((group, SIDE, slots, JP, C), lambda g: (g, 0, 0, 0, 0)),
        ],
        out_specs=pl.BlockSpec((C, COLS), lambda g: (0, 0), pipeline_mode=pl.Buffered(1)),
        scratch_shapes=[
            pltpu.VMEM((23, group, 32, 128), F32),
            pltpu.VMEM((22 * group * JP, PAIR), BF16),
            pltpu.VMEM((SIDE, group, JP, C), F32),
            pltpu.VMEM((C, COLS), F32),
        ],
        compiler_params=pltpu.CompilerParams(vmem_limit_bytes=LIMIT),
        cost_estimate=cost(groups * one_product // 2),
        name="dictionary",
    )(filters, everyone)

    def flat(array):
        return array[:, :, 0:SIDE, :].transpose(1, 0, 2, 3).reshape(slots, SIDE * SIDE * M)

    return flat(codes), flat(duals), new_filters


def solution(mesh):
    return jax.shard_map(
        local,
        mesh=mesh,
        in_specs=(
            P(("runs", "tile"), None, None),
            P(("runs", "tile")),
            P(),
            P(("runs", "tile"), None),
            P(("runs", "tile"), None),
        ),
        out_specs=(P(("runs", "tile"), None), P(("runs", "tile"), None), P("runs", None)),
        check_vma=False,
    )
```

time: 542 us -> 114 us (0.21); the launches traced: 532 us -> 113 us
  local copies, waits for them, and re-layouts: 350 us -> 17.7 us
  waiting for transfers between devices: 91.9 us -> 40.2 us
  Pallas kernels: 0 us -> 41.3 us
  blocking collectives: 32.2 us -> 0 us
  matrix products: 27.8 us -> 0 us
  other arithmetic: 12.6 us -> 0 us
    unnamed x469 -> x9, local copies, waits for them, and re-layouts: 172 us -> 12.8 us
    reduce_scatter x1 -> x0, waiting for transfers between devices: 80.3 us -> none  [dictionary_step(): lax.psum_scatter(term_maker(residual, patches), 'tile', scatter_dimension...]
    slice x15 -> x0, local copies, waits for them, and re-layouts: 59.8 us -> none  [fold_back(): piece = shaped[:, :, :, row_off * K + col_off, :].astype(jnp.float32)]
    reshape x6 -> x7, local copies, waits for them, and re-layouts: 54.6 us -> 1.77 us  [the longest x2 1.49 us: flat(): array[:, :, 0:SIDE, :].transpose(1, 0, 2, 3).reshape(slots, SIDE * SIDE * M)]
    pallas_call x0 -> x3, Pallas kernels: none -> 41.3 us  [the longest x1 23.4 us: local(): pl.pallas_call(lambda *refs: dictionary_kernel(stride, *refs), grid=(grou...]
    convert_element_type x62 -> x0, local copies, waits for them, and re-layouts: 32.7 us -> none  [the longest x60 31.7 us: fold_back(): piece = shaped[:, :, :, row_off * K + col_off, :].astype(jnp.float32)]
    psum x1 -> x0, blocking collectives: 32.2 us -> none  [dictionary_step(): totals = lax.psum(squares, 'tile')]
    another operation x4 -> x0, local copies, waits for them, and re-layouts: 29 us -> none  [patches_of(): return jnp.stack(columns, axis=3).reshape(number * SIDE * SIDE, K * K * M)]
  transfers between devices with their start and end apart: 2 -> 1, of which waited for: 2 -> 1; matrix products, arithmetic and copies ran while one was open for 11% -> 2% of each run, Pallas kernels for 0% -> 5%
where the time goes in v1:
time: 114 us; the launch traced here: 113 us
  Pallas kernels  41.3 us (36%)
  waiting for transfers between devices  40.2 us (35%)
  local copies, waits for them, and re-layouts  17.7 us (16%)
  between operations  14.1 us (12%)
    all_gather x1, waiting for transfers between devices, local(): everyone = lax.all_gather(payload, 'tile', axis=0)  40.2 us
    pallas_call x1, Pallas kernels, local(): pl.pallas_call(lambda *refs: dictionary_kernel(stride, *refs), grid=(grou...  23.4 us
    unnamed x9, local copies, waits for them, and re-layouts  12.8 us
    pallas_call x1, Pallas kernels, local(): pl.pallas_call(first_kernel, out_shape=(jax.ShapeDtypeStruct((SIDE, slots...  12.6 us
    pallas_call x1, Pallas kernels, local(): pl.pallas_call(second_kernel, out_shape=(state, state), in_specs=[in_vmem...  5.31 us
  transfers between devices with their start and end apart: 1, of which 1 were waited for; matrix products, arithmetic and copies ran while one was open for 2% of the time, Pallas kernels for 5%

profile of v1, /device:TPU:0, one launch (start us, length us, event | category | flops | bytes accessed | tf_op | source)
XLA Modules:
  0.0 113.3 jit_solution(444656882897595484)
XLA Ops:
  7.2 0.0 copy-start
  7.2 0.0 copy-start.1
  7.2 0.0 copy-start.2
  7.2 0.0 all-gather.3.cloned.1.call-start
  7.2 6.3 %copy.27.f_ref.refs_0_ = bf16[256,7744]{1,0:T(8,128)(2,1)} copy(bf16[256,7744]{0,1:T(8,128)(2,1)} %param.7) | data formatting | bytes 7929856 | tf_op args[2]
  13.6 0.0 copy-done
  13.6 0.1 copy.22
  13.7 0.0 copy-done.1
  13.7 0.1 reshape.22
  13.9 0.7 pad.11.img_ref
  14.6 0.7 pad.12.codes_ref
  15.3 0.0 copy-done.2
  15.3 0.1 reshape.23
  15.4 0.7 pad.13.duals_ref
  16.1 12.6 %first_pass.1 = (bf16[12,2,16,256]{3,2,1,0:T(8,128)(2,1)}, f32[12,2,16,64]{3,2,1,0:T(8,128)}, f32[12,2,16,64]{3,2,1,0:T(8,128)}) custom-call(s32[2]{0:T(128)} %rows_ref.1, bf16[256,7744]{1,0:T(8,128)(2,1)} %copy.27.f_ref.refs_0_, bf16[12,2,16,256]{3,2,1,0:T(8,128)(2,1)} %pad.11.img_ref, bf16[12,2,16,64]{3,2,1,0:T(8,128)(2,1)} %pad.12.codes_ref, ...), custom_call_target="tpu_custom_call" | custom-call | flops 3425697792 | bytes 8388608 | tf_op jit(solution)/shard_map/first_pass/pallas_call | solution.py:269
  28.7 0.0 all-gather.3.cloned.1.call-update
  28.7 5.3 %second_codes.1 = (f32[12,2,16,64]{3,2,1,0:T(8,128)}, f32[12,2,16,64]{3,2,1,0:T(8,128)}) custom-call(bf16[256,7744]{1,0:T(8,128)(2,1)} %copy.27.f_ref.refs_0_, bf16[12,2,16,256]{3,2,1,0:T(8,128)(2,1)} %get-tuple-element.8.pay_ref, f32[12,2,16,64]{3,2,1,0:T(8,128)} %get-tuple-element.9.codes_ref, f32[12,2,16,64]{3,2,1,0:T(8,128)} %get-tuple-element.10.duals_ref), custom_call_target="tpu_custom_call" | custom-call | flops 1141899264 | bytes 8388608 | tf_op jit(solution)/shard_map/second_codes/pallas_call | solution.py:291
  34.0 1.0 slice_bitcast_fusion
  35.1 0.7 reshape.24
  35.8 0.7 reshape.25
  36.6 40.2 %all-gather.3.cloned.1.call-done = bf16[192,2,16,256]{3,2,1,0:T(8,128)(2,1)} async-done(((bf16[12,2,16,256]{3,2,1,0:T(8,128)(2,1)}), bf16[192,2,16,256]{3,2,1,0:T(8,128)(2,1)}) %all-gather.3.cloned.1.call-update) | async-done | bytes 3145744 | tf_op jit(solution)/shard_map/all_gather | solution.py:290
  76.7 23.4 %dictionary.1 = bf16[256,7744]{1,0:T(8,128)(2,1)} custom-call(bf16[256,7744]{1,0:T(8,128)(2,1)} %copy.27.f_ref.refs_0_, bf16[16,12,2,16,256]{4,3,2,1,0:T(8,128)(2,1)} %bitcast.19), custom_call_target="tpu_custom_call" | custom-call | flops 9135194112 | bytes 8388608 | tf_op jit(solution)/shard_map/dictionary/pallas_call | solution.py:302
  100.1 6.3 %copy.31 = bf16[256,7744]{0,1:T(8,128)(2,1)} copy(bf16[256,7744]{1,0:T(8,128)(2,1)} %dictionary.1) | data formatting | bytes 7929856
  (5 shorter events, 0.1 us)
Async XLA Ops:
  7.2 6.4 %copy-start = (bf16[2,144,256]{2,1,0:T(8,128)(2,1)S(1)}, bf16[2,144,256]{2,1,0:T(8,128)(2,1)}, u32[]{:S(2)}) copy-start(bf16[2,144,256]{2,1,0:T(8,128)(2,1)} %param.5) | copy-start | bytes 442372
  7.2 6.6 %copy-start.1 = (bf16[2,9216]{1,0:T(2,128)(2,1)S(1)}, bf16[2,9216]{1,0:T(2,128)(2,1)}, u32[]{:S(2)}) copy-start(bf16[2,9216]{1,0:T(2,128)(2,1)} %param.8) | copy-start | bytes 110596
  7.2 8.1 %copy-start.2 = (bf16[2,9216]{1,0:T(2,128)(2,1)S(1)}, bf16[2,9216]{1,0:T(2,128)(2,1)}, u32[]{:S(2)}) copy-start(bf16[2,9216]{1,0:T(2,128)(2,1)} %param.9) | copy-start | bytes 110596
  7.2 69.5 %all-gather.3.cloned.1.call-start = ((), (), s32[]{:S(2)}) async-start(), calls=%async_computation | async-start | bytes 3342336 | tf_op jit(solution)/shard_map/all_gather | solution.py:290
Sparse Core Ops, SparseCore 0:
  28.8 47.8 all-gather.2

commit v2 on v1

--- a/solution.py
+++ b/solution.py
@@ -58,8 +58,8 @@
         at = p * 2 * slots * JP
         part = lax.dot_general(
             taps[at : at + rows, 0:width],
-            f_ref[:, p * PAIR : p * PAIR + width],
-            (((1,), (1,)), ((), ())),
+            f_ref[p * PAIR : p * PAIR + width, :],
+            (((1,), (0,)), ((), ())),
             preferred_element_type=F32,
         )
         total = part if total is None else total + part
@@ -68,7 +68,7 @@
 
 def fill_tail(f_ref, ftail):
     ftail[...] = jnp.zeros_like(ftail)
-    ftail[:, 0:192] = f_ref[:, COLS - 192 : COLS]
+    ftail[0:192, :] = f_ref[COLS - 192 : COLS, :]
 
 
 def code_gradient(rpad, f_ref, ftail, zpad, slots):
@@ -79,15 +79,18 @@
         acc = None
         for p in range(6):
             at = (10 - 2 * p) * step
-            if p < 5:
-                piece = f_ref[:, p * PAIR + n * 256 : p * PAIR + n * 256 + width]
-            elif n < 2:
-                piece = f_ref[:, p * PAIR + n * 256 : p * PAIR + n * 256 + width]
+            if p < 5 or n < 2:
+                piece = f_ref[p * PAIR + n * 256 : p * PAIR + n * 256 + width, :]
             elif n == 2:
                 piece = ftail[...]
             else:
                 continue
-            part = jnp.dot(rpad[at : at + rows, :], piece, preferred_element_type=F32)
+            part = lax.dot_general(
+                rpad[at : at + rows, :],
+                piece,
+                (((1,), (1,)), ((), ())),
+                preferred_element_type=F32,
+            )
             acc = part if acc is None else acc + part
         for h in range(width // 128):
             zpad[2 * n + h, :, :, 8:24, :] = acc[:, h * 128 : (h + 1) * 128].reshape(
@@ -186,14 +189,17 @@
     duals_out[...] = duals
 
 
-def dictionary_kernel(stride, f_ref, all_ref, new_ref, dpad, taps, stage, total):
+def dictionary_kernel(stride, f_ref, all_ref, new_ref, maps, taps, stage, total):
     at = pl.program_id(0)
     group = all_ref.shape[0]
-    rows = SIDE * group * JP
+    row = group * JP
+    rows = SIDE * row
+    edge = (K - 1) // 2
 
     @pl.when(at == 0)
     def _():
-        dpad[...] = jnp.zeros_like(dpad)
+        maps[...] = jnp.zeros_like(maps)
+        taps[...] = jnp.zeros_like(taps)
         total[...] = jnp.zeros_like(total)
 
     for d in range(0, group, 2):
@@ -202,41 +208,43 @@
                 d + 1, :, 1 - k, :, :
             ].astype(F32)
     for k in range(3):
-        lanes = slice(k * M, (k + 1) * M)
-        codes = stage[:, :, SIDE:JP, lanes]
-        both = jnp.concatenate([codes, codes], axis=-1)
-        dpad[5 : 5 + SIDE, :, 6 + 4 * k : 10 + 4 * k, 0:M] = both[..., 0:M]
-        dpad[5 : 5 + SIDE, :, 5 + 4 * k : 9 + 4 * k, M : 2 * M] = both[..., M : 2 * M]
-    build_taps(dpad, taps)
+        maps[:, :, 4 * k : 4 * k + 4, :] = stage[:, :, SIDE:JP, k * M : (k + 1) * M]
+    col = lax.broadcasted_iota(jnp.int32, (M, row), 1) % JP
+    for i in range(SIDE):
+        turned = maps[i].reshape(row, M).T
+        for b in range(K):
+            moved = turned if b == edge else pltpu.roll(turned, (edge - b) % row, 1)
+            if b == 0:
+                moved = jnp.where(col == 0, 0.0, moved)
+            if b == K - 1:
+                moved = jnp.where(col == SIDE - 1, 0.0, moved)
+            taps[b * M : (b + 1) * M, (i + edge) * row : (i + edge + 1) * row] = moved.astype(BF16)
     values = stage[...]
-    col = lax.broadcasted_iota(jnp.int32, values.shape, 2)
-    turned = jnp.where(col < SIDE, values, 0.0).reshape(rows, C).T.astype(BF16)
-    for p in range(6):
-        width = PAIR if p < 5 else LAST
-        start = p * 2 * group * JP
-        total[:, p * PAIR : p * PAIR + width] += jnp.dot(
-            turned, taps[start : start + rows, 0:width], preferred_element_type=F32
+    place = lax.broadcasted_iota(jnp.int32, values.shape, 2)
+    residual = jnp.where(place < SIDE, values, 0.0).reshape(rows, C).astype(BF16)
+    for a in range(K):
+        total[a * LAST : (a + 1) * LAST, :] += jnp.dot(
+            taps[:, a * row : a * row + rows], residual, preferred_element_type=F32
         )
 
     @pl.when(at == pl.num_programs(0) - 1)
     def _():
-        squares = jnp.zeros((C, 128), F32)
-        for q in range(COLS // 128 + 1):
-            width = min(128, COLS - q * 128)
-            lanes = slice(q * 128, q * 128 + width)
-            moved = f_ref[:, lanes].astype(F32) - (stride * FACTOR) * total[:, lanes]
-            total[:, lanes] = moved
-            if width == 128:
-                squares = squares + moved * moved
-        tail = jnp.sum(moved * moved, axis=0, keepdims=True)
-        sums = jnp.sum(squares, axis=0, keepdims=True)
-        each = sums[:, 0:M] + sums[:, M : 2 * M] + tail
-        inverse = 1.0 / jnp.sqrt(each / (C * K * K) + EPSILON)
-        wide = jnp.concatenate([inverse, inverse], axis=-1)
-        for q in range(COLS // 128 + 1):
-            width = min(128, COLS - q * 128)
-            lanes = slice(q * 128, q * 128 + width)
-            new_ref[:, lanes] = (total[:, lanes] * wide[:, 0:width]).astype(BF16)
+        def step(t, squares):
+            part = pl.ds(pl.multiple_of(t * M, M), M)
+            moved = f_ref[part, :].astype(F32) - (stride * FACTOR) * total[part, :]
+            total[part, :] = moved
+            return squares + moved * moved
+
+        squares = lax.fori_loop(0, K * K, step, jnp.zeros((M, C), F32), unroll=11)
+        sums = jnp.sum(squares, axis=1, keepdims=True)
+        inverse = 1.0 / jnp.sqrt(sums / (C * K * K) + EPSILON)
+
+        def scale(t, carry):
+            part = pl.ds(pl.multiple_of(t * M, M), M)
+            new_ref[part, :] = (total[part, :] * inverse).astype(BF16)
+            return carry
+
+        lax.fori_loop(0, K * K, scale, 0, unroll=11)
 
 
 def in_vmem():
@@ -263,7 +271,7 @@
     one_product = 2 * SIDE * SIDE * slots * C * COLS
     back = [
         pltpu.VMEM((23 * slots * JP, C), BF16),
-        pltpu.VMEM((C, 256), BF16),
+        pltpu.VMEM((256, C), BF16),
         pltpu.VMEM((BLOCKS, 13, slots, 40, 128), F32),
     ]
     payload, codes_mid, duals_mid = pl.pallas_call(
@@ -282,7 +290,7 @@
         name="first_pass",
     )(
         tissue_rows,
-        filters,
+        filters.T,
         arranged(image_stack, C),
         arranged(codes_start, M),
         arranged(duals_start, M),
@@ -297,32 +305,33 @@
         compiler_params=pltpu.CompilerParams(vmem_limit_bytes=LIMIT),
         cost_estimate=cost(one_product),
         name="second_codes",
-    )(filters, payload, codes_mid, duals_mid)
-    group = 4 if groups % 4 == 0 else 2
+    )(filters.T, payload, codes_mid, duals_mid)
+    group = 8
+    columns = filters.T
     new_filters = pl.pallas_call(
         lambda *refs: dictionary_kernel(stride, *refs),
         grid=(groups // group,),
-        out_shape=jax.ShapeDtypeStruct((C, COLS), BF16),
+        out_shape=jax.ShapeDtypeStruct((COLS, C), BF16),
         in_specs=[
-            pl.BlockSpec((C, COLS), lambda g: (0, 0), pipeline_mode=pl.Buffered(1)),
+            pl.BlockSpec((COLS, C), lambda g: (0, 0), pipeline_mode=pl.Buffered(1)),
             pl.BlockSpec((group, SIDE, slots, JP, C), lambda g: (g, 0, 0, 0, 0)),
         ],
-        out_specs=pl.BlockSpec((C, COLS), lambda g: (0, 0), pipeline_mode=pl.Buffered(1)),
+        out_specs=pl.BlockSpec((COLS, C), lambda g: (0, 0), pipeline_mode=pl.Buffered(1)),
         scratch_shapes=[
-            pltpu.VMEM((23, group, 32, 128), F32),
-            pltpu.VMEM((22 * group * JP, PAIR), BF16),
+            pltpu.VMEM((SIDE, group, JP, M), F32),
+            pltpu.VMEM((LAST, 22 * group * JP), BF16),
             pltpu.VMEM((SIDE, group, JP, C), F32),
-            pltpu.VMEM((C, COLS), F32),
+            pltpu.VMEM((COLS, C), F32),
         ],
         compiler_params=pltpu.CompilerParams(vmem_limit_bytes=LIMIT),
         cost_estimate=cost(groups * one_product // 2),
         name="dictionary",
-    )(filters, everyone)
+    )(columns, everyone)
 
     def flat(array):
         return array[:, :, 0:SIDE, :].transpose(1, 0, 2, 3).reshape(slots, SIDE * SIDE * M)
 
-    return flat(codes), flat(duals), new_filters
+    return flat(codes), flat(duals), new_filters.T
 
 
 def solution(mesh):

time: 114 us -> 101 us (0.89)
  local copies, waits for them, and re-layouts: 17.7 us -> 7.42 us
  Pallas kernels: 41.3 us -> 38.8 us
    unnamed x9 -> x1, local copies, waits for them, and re-layouts: 12.8 us -> 1.02 us
    pallas_call x1, Pallas kernels: 23.4 us -> 21 us  [local(): pl.pallas_call(lambda *refs: dictionary_kernel(stride, *refs), grid=(grou...]
    reshape x5, local copies, waits for them, and re-layouts: 0.28 us -> 1.81 us  [arranged(): shaped = array.reshape(slots, SIDE, SIDE, width).transpose(1, 0, 2, 3)]
  transfers between devices with their start and end apart: 1 -> 1, of which waited for: 1 -> 1; matrix products, arithmetic and copies ran while one was open for 2% -> 3% of each run, Pallas kernels for 5% -> 5%
where the time goes in v2:
time: 101 us
  waiting for transfers between devices  40.2 us (40%)
  Pallas kernels  38.8 us (38%)
  between operations  14.1 us (14%)
  local copies, waits for them, and re-layouts  7.42 us (7%)
    all_gather x1, waiting for transfers between devices, local(): everyone = lax.all_gather(payload, 'tile', axis=0)  40.2 us
    pallas_call x1, Pallas kernels, local(): pl.pallas_call(lambda *refs: dictionary_kernel(stride, *refs), grid=(grou...  21 us
    pallas_call x1, Pallas kernels, local(): pl.pallas_call(first_kernel, out_shape=(jax.ShapeDtypeStruct((SIDE, slots...  12.6 us
    pallas_call x1, Pallas kernels, local(): pl.pallas_call(second_kernel, out_shape=(state, state), in_specs=[in_vmem...  5.25 us
  transfers between devices with their start and end apart: 1, of which 1 were waited for; matrix products, arithmetic and copies ran while one was open for 3% of the time, Pallas kernels for 5%

profile of v2, /device:TPU:0, one launch (start us, length us, event | category | flops | bytes accessed | tf_op | source)
XLA Modules:
  0.0 100.6 jit_solution(11829887129844679944)
XLA Ops:
  7.2 0.0 all-gather.3.cloned.1.call-start
  7.2 0.9 reshape.22
  8.1 0.9 reshape.23
  9.0 0.7 pad.12.codes_ref
  9.7 0.7 pad.13.duals_ref
  10.3 1.0 %copy.14 = bf16[2,144,256]{2,0,1:T(2,128)(2,1)S(1)} copy(bf16[2,144,256]{2,1,0:T(8,128)(2,1)} %param.5) | data formatting | bytes 294912 | tf_op args[0]
  11.4 0.7 pad.11.img_ref
  12.1 12.6 %first_pass.1 = (bf16[12,2,16,256]{3,2,1,0:T(8,128)(2,1)}, f32[12,2,16,64]{3,2,1,0:T(8,128)}, f32[12,2,16,64]{3,2,1,0:T(8,128)}) custom-call(s32[2]{0:T(128)} %rows_ref.1, bf16[7744,256]{1,0:T(8,128)(2,1)} %bitcast.17, bf16[12,2,16,256]{3,2,1,0:T(8,128)(2,1)} %pad.11.img_ref, bf16[12,2,16,64]{3,2,1,0:T(8,128)(2,1)} %pad.12.codes_ref, ...), custom_call_target="tpu_custom_call" | custom-call | flops 3425697792 | bytes 8388608 | tf_op jit(solution)/shard_map/first_pass/pallas_call | solution.py:277
  24.7 0.0 all-gather.3.cloned.1.call-update
  24.7 5.3 %second_codes.1 = (f32[12,2,16,64]{3,2,1,0:T(8,128)}, f32[12,2,16,64]{3,2,1,0:T(8,128)}) custom-call(bf16[7744,256]{1,0:T(8,128)(2,1)} %bitcast.18, bf16[12,2,16,256]{3,2,1,0:T(8,128)(2,1)} %get-tuple-element.8.pay_ref, f32[12,2,16,64]{3,2,1,0:T(8,128)} %get-tuple-element.9.codes_ref, f32[12,2,16,64]{3,2,1,0:T(8,128)} %get-tuple-element.10.duals_ref), custom_call_target="tpu_custom_call" | custom-call | flops 1141899264 | bytes 8388608 | tf_op jit(solution)/shard_map/second_codes/pallas_call | solution.py:299
  29.9 1.0 %slice_bitcast_fusion = (f32[2,12,12,64]{3,2,0,1:T(8,128)S(1)}, f32[2,12,12,64]{3,2,0,1:T(8,128)S(1)}) fusion(f32[12,2,16,64]{3,2,1,0:T(8,128)} %get-tuple-element.12, f32[12,2,16,64]{3,2,1,0:T(8,128)} %get-tuple-element.11), kind=kLoop, calls=%fused_computation.1 | loop fusion | bytes 294912 | tf_op jit(solution)/shard_map/transpose | solution.py:332
  31.0 0.7 reshape.25
  31.8 0.7 reshape.24
  32.5 40.2 %all-gather.3.cloned.1.call-done = bf16[192,2,16,256]{3,2,1,0:T(8,128)(2,1)} async-done(((bf16[12,2,16,256]{3,2,1,0:T(8,128)(2,1)}), bf16[192,2,16,256]{3,2,1,0:T(8,128)(2,1)}) %all-gather.3.cloned.1.call-update) | async-done | bytes 3145744 | tf_op jit(solution)/shard_map/all_gather | solution.py:298
  72.7 21.0 %dictionary.1 = bf16[7744,256]{1,0:T(8,128)(2,1)} custom-call(bf16[7744,256]{1,0:T(8,128)(2,1)} %bitcast.19, bf16[16,12,2,16,256]{4,3,2,1,0:T(8,128)(2,1)} %bitcast.24), custom_call_target="tpu_custom_call" | custom-call | flops 9135194112 | bytes 8388608 | tf_op jit(solution)/shard_map/dictionary/pallas_call | solution.py:311
  (5 shorter events, 0.1 us)
Async XLA Ops:
  7.2 65.6 %all-gather.3.cloned.1.call-start = ((), (), s32[]{:S(2)}) async-start(), calls=%async_computation | async-start | bytes 3342336 | tf_op jit(solution)/shard_map/all_gather | solution.py:298
Sparse Core Ops, SparseCore 0:
  24.8 47.8 all-gather.2

commit v3 on v2

--- a/solution.py
+++ b/solution.py
@@ -169,24 +169,105 @@
     held = jnp.where(occupied[..., 0:M], codes, 0.0)
     for k in range(3):
         stage[:, :, SIDE:JP, k * M : (k + 1) * M] = held[:, :, 4 * k : 4 * k + 4, :]
-    pay_ref[...] = stage[...].astype(BF16)
+    for s in range(slots):
+        pay_ref[s] = stage[:, s, :, :].astype(BF16)
 
 
 def second_kernel(f_ref, pay_ref, codes_ref, duals_ref, codes_out, duals_out, rpad, ftail, zpad):
-    slots = pay_ref.shape[1]
-    rows = SIDE * slots * JP
-    lead = 6 * slots * JP
+    slots = pay_ref.shape[0]
     rpad[...] = jnp.zeros_like(rpad)
     zpad[...] = jnp.zeros_like(zpad)
     fill_tail(f_ref, ftail)
-    payload = pay_ref[...].astype(F32)
-    col = lax.broadcasted_iota(jnp.int32, payload.shape, 2)
-    residual = jnp.where(col < SIDE, payload, 0.0)
-    rpad[lead : lead + rows, :] = residual.reshape(rows, C).astype(BF16)
+    for s in range(slots):
+        payload = pay_ref[s].astype(F32)
+        col = lax.broadcasted_iota(jnp.int32, payload.shape, 1)
+        residual = jnp.where(col < SIDE, payload, 0.0).astype(BF16)
+        for i in range(SIDE):
+            at = ((6 + i) * slots + s) * JP
+            rpad[at : at + JP, :] = residual[i]
     gradient = code_gradient(rpad, f_ref, ftail, zpad, slots)
     codes, duals = admm_update(codes_ref[...], duals_ref[...], gradient)
     codes_out[...] = codes
     duals_out[...] = duals
+
+
+MESH = pl.DeviceIdType.MESH
+
+
+def gather_kernel(
+    outer, inner, pay_ref, all_ref, other, pair_send, pair_recv, z_send, z_recv,
+    y_send, y_recv, c_send, c_recv
+):
+    me = lax.axis_index("tile")
+    core = lax.rem(me, 2)
+    inn = lax.rem(me // 2, inner)
+    out = me // (2 * inner)
+
+    def index(dz, dy, c):
+        return (lax.rem(out + dz + outer, outer) * inner + lax.rem(inn + dy + inner, inner)) * 2 + c
+
+    partner = index(0, 0, 1 - core)
+    barrier = pltpu.get_barrier_semaphore()
+    peers = [index(dz, 0, core) for dz in range(1, outer)]
+    peers += [index(0, dy, core) for dy in range(1, inner)] + [partner]
+    for peer in peers:
+        pl.semaphore_signal(barrier, inc=1, device_id={"tile": peer}, device_id_type=MESH)
+    pl.semaphore_wait(barrier, len(peers))
+
+    def copy(src, dst, send, recv, target):
+        return pltpu.make_async_remote_copy(
+            src_ref=src,
+            dst_ref=dst,
+            send_sem=send,
+            recv_sem=recv,
+            device_id={"tile": target},
+            device_id_type=MESH,
+        )
+
+    swap = copy(pay_ref.at[1], other, pair_send, pair_recv, partner)
+    swap.start()
+    swap.wait()
+    all_ref[me] = (pay_ref[0].astype(F32) + other[...].astype(F32)).astype(BF16)
+
+    started = []
+
+    def along_z(dz):
+        return copy(all_ref.at[me], all_ref.at[me], z_send.at[dz], z_recv.at[dz], index(dz, 0, core))
+
+    def along_y(dz, dy):
+        block = all_ref.at[index(-dz, 0, core)]
+        return copy(block, block, y_send.at[dz, dy], y_recv.at[dz, dy], index(0, dy, core))
+
+    def across(dz, dy):
+        block = all_ref.at[index(-dz, -dy, core)]
+        return copy(block, block, c_send.at[dz, dy], c_recv.at[dz, dy], partner)
+
+    def start(one):
+        one.start()
+        started.append(one)
+
+    def arrived(block, recv, send):
+        copy(block, block, send, recv, partner).wait_recv()
+
+    for dz in range(1, outer):
+        start(along_z(dz))
+    for dy in range(1, inner):
+        start(along_y(0, dy))
+    start(across(0, 0))
+    for dz in range(1, outer):
+        arrived(all_ref.at[index(-dz, 0, core)], z_recv.at[dz], z_send.at[dz])
+        for dy in range(1, inner):
+            start(along_y(dz, dy))
+        start(across(dz, 0))
+    for dz in range(outer):
+        for dy in range(1, inner):
+            arrived(all_ref.at[index(-dz, -dy, core)], y_recv.at[dz, dy], y_send.at[dz, dy])
+            start(across(dz, dy))
+    for dz in range(outer):
+        for dy in range(inner):
+            arrived(all_ref.at[index(-dz, -dy, 1 - core)], c_recv.at[dz, dy], c_send.at[dz, dy])
+    for one in started:
+        one.wait_send()
 
 
 def dictionary_kernel(stride, f_ref, all_ref, new_ref, maps, taps, stage, total):
@@ -202,11 +283,8 @@
         taps[...] = jnp.zeros_like(taps)
         total[...] = jnp.zeros_like(total)
 
-    for d in range(0, group, 2):
-        for k in range(2):
-            stage[:, d + k, :, :] = all_ref[d, :, k, :, :].astype(F32) + all_ref[
-                d + 1, :, 1 - k, :, :
-            ].astype(F32)
+    for d in range(group):
+        stage[:, d, :, :] = all_ref[d].astype(F32)
     for k in range(3):
         maps[:, :, 4 * k : 4 * k + 4, :] = stage[:, :, SIDE:JP, k * M : (k + 1) * M]
     col = lax.broadcasted_iota(jnp.int32, (M, row), 1) % JP
@@ -276,7 +354,7 @@
     ]
     payload, codes_mid, duals_mid = pl.pallas_call(
         first_kernel,
-        out_shape=(jax.ShapeDtypeStruct((SIDE, slots, JP, C), BF16), state, state),
+        out_shape=(jax.ShapeDtypeStruct((slots, SIDE, JP, C), BF16), state, state),
         in_specs=[pl.BlockSpec(memory_space=pltpu.SMEM)] + [in_vmem()] * 4,
         out_specs=(in_vmem(),) * 3,
         scratch_shapes=[
@@ -295,7 +373,32 @@
         arranged(codes_start, M),
         arranged(duals_start, M),
     )
-    everyone = lax.all_gather(payload, "tile", axis=0)
+    chips = groups // 2
+    inner = 1 << ((chips.bit_length() - 1) // 2)
+    outer = chips // inner
+    dma = pltpu.SemaphoreType.DMA
+    everyone = pl.pallas_call(
+        lambda *refs: gather_kernel(outer, inner, *refs),
+        out_shape=jax.ShapeDtypeStruct((groups, SIDE, JP, C), BF16),
+        in_specs=[in_vmem()],
+        out_specs=in_vmem(),
+        scratch_shapes=[
+            pltpu.VMEM((SIDE, JP, C), BF16),
+            dma,
+            dma,
+            dma((outer,)),
+            dma((outer,)),
+            dma((outer, inner)),
+            dma((outer, inner)),
+            dma((outer, inner)),
+            dma((outer, inner)),
+        ],
+        compiler_params=pltpu.CompilerParams(
+            vmem_limit_bytes=LIMIT, collective_id=0, has_side_effects=True
+        ),
+        cost_estimate=cost(1),
+        name="gather_slots",
+    )(payload)
     codes, duals = pl.pallas_call(
         second_kernel,
         out_shape=(state, state),
@@ -314,7 +417,7 @@
         out_shape=jax.ShapeDtypeStruct((COLS, C), BF16),
         in_specs=[
             pl.BlockSpec((COLS, C), lambda g: (0, 0), pipeline_mode=pl.Buffered(1)),
-            pl.BlockSpec((group, SIDE, slots, JP, C), lambda g: (g, 0, 0, 0, 0)),
+            pl.BlockSpec((group, SIDE, JP, C), lambda g: (g, 0, 0, 0)),
         ],
         out_specs=pl.BlockSpec((COLS, C), lambda g: (0, 0), pipeline_mode=pl.Buffered(1)),
         scratch_shapes=[

time: 101 us -> 71.4 us (0.71)
  waiting for transfers between devices: 40.2 us -> 0 us
  Pallas kernels: 38.8 us -> 63 us
  between operations: 14.1 us -> 0.69 us
    all_gather x1 -> x0, waiting for transfers between devices: 40.2 us -> none  [local(): everyone = lax.all_gather(payload, 'tile', axis=0)]
    pallas_call x1 -> x2, Pallas kernels: 12.6 us -> 36.7 us  [the longest x1 24.2 us: local(): pl.pallas_call(lambda *refs: gather_kernel(outer, inner, *refs), out_shap...]
  transfers between devices with their start and end apart: 1 -> 0, of which waited for: 1 -> 0; matrix products, arithmetic and copies ran while one was open for 3% -> 0% of each run, Pallas kernels for 5% -> 0%
where the time goes in v3:
time: 71.4 us; the launch traced here: 71.1 us
  Pallas kernels  63 us (88%)
  local copies, waits for them, and re-layouts  7.42 us (10%)
    pallas_call x1, Pallas kernels, local(): pl.pallas_call(lambda *refs: gather_kernel(outer, inner, *refs), out_shap...  24.2 us
    pallas_call x1, Pallas kernels, local(): pl.pallas_call(lambda *refs: dictionary_kernel(stride, *refs), grid=(grou...  21 us
    pallas_call x1, Pallas kernels, local(): pl.pallas_call(first_kernel, out_shape=(jax.ShapeDtypeStruct((slots, SIDE...  12.6 us
    pallas_call x1, Pallas kernels, local(): pl.pallas_call(second_kernel, out_shape=(state, state), in_specs=[in_vmem...  5.26 us
    pad x3, local copies, waits for them, and re-layouts, arranged(): return jnp.pad(shaped, ((0, 0), (0, 0), (0, JP - SIDE), (0, 0)))  2.02 us
    reshape x5, local copies, waits for them, and re-layouts, arranged(): shaped = array.reshape(slots, SIDE, SIDE, width).transpose(1, 0, 2, 3)  1.81 us
    reshape x2, local copies, waits for them, and re-layouts, flat(): array[:, :, 0:SIDE, :].transpose(1, 0, 2, 3).reshape(slots, SIDE * SIDE * M)  1.49 us

profile of v3, /device:TPU:0, one launch (start us, length us, event | category | flops | bytes accessed | tf_op | source)
XLA Modules:
  0.0 71.1 jit_solution(11767894176779740669)
XLA Ops:
  0.6 0.9 %reshape.22 = bf16[2,12,12,64]{3,2,1,0:T(8,128)(2,1)S(1)} reshape(bf16[2,9216]{1,0:T(2,128)(2,1)} %param.8) | data formatting | bytes 73728 | tf_op jit(solution)/shard_map/reshape | solution.py:345
  1.5 0.7 pad.12.codes_ref
  2.2 0.9 %reshape.23 = bf16[2,12,12,64]{3,2,1,0:T(8,128)(2,1)S(1)} reshape(bf16[2,9216]{1,0:T(2,128)(2,1)} %param.9) | data formatting | bytes 73728 | tf_op jit(solution)/shard_map/reshape | solution.py:345
  3.1 0.7 pad.13.duals_ref
  3.8 1.0 %copy.8 = bf16[2,144,256]{2,0,1:T(2,128)(2,1)S(1)} copy(bf16[2,144,256]{2,1,0:T(8,128)(2,1)} %param.5) | data formatting | bytes 294912 | tf_op args[0]
  4.8 0.7 pad.11.img_ref
  5.5 12.6 %first_pass.1 = (bf16[2,12,16,256]{3,2,1,0:T(8,128)(2,1)}, f32[12,2,16,64]{3,2,1,0:T(8,128)}, f32[12,2,16,64]{3,2,1,0:T(8,128)}) custom-call(s32[2]{0:T(128)} %rows_ref.1, bf16[7744,256]{1,0:T(8,128)(2,1)} %bitcast.16, bf16[12,2,16,256]{3,2,1,0:T(8,128)(2,1)} %pad.11.img_ref, bf16[12,2,16,64]{3,2,1,0:T(8,128)(2,1)} %pad.12.codes_ref, ...), custom_call_target="tpu_custom_call" | custom-call | flops 3425697792 | bytes 8388608 | tf_op jit(solution)/shard_map/first_pass/pallas_call | solution.py:355
  18.1 5.3 %second_codes.1 = (f32[12,2,16,64]{3,2,1,0:T(8,128)}, f32[12,2,16,64]{3,2,1,0:T(8,128)}) custom-call(bf16[7744,256]{1,0:T(8,128)(2,1)} %bitcast.17, bf16[2,12,16,256]{3,2,1,0:T(8,128)(2,1)} %get-tuple-element.8.pay_ref.refs_0_, f32[12,2,16,64]{3,2,1,0:T(8,128)} %get-tuple-element.9.codes_ref, f32[12,2,16,64]{3,2,1,0:T(8,128)} %get-tuple-element.10.duals_ref), custom_call_target="tpu_custom_call" | custom-call | flops 1141899264 | bytes 8388608 | tf_op jit(solution)/shard_map/second_codes/pallas_call | solution.py:402
  23.4 1.0 %slice_bitcast_fusion = (f32[2,12,12,64]{3,2,0,1:T(8,128)S(1)}, f32[2,12,12,64]{3,2,0,1:T(8,128)S(1)}) fusion(f32[12,2,16,64]{3,2,1,0:T(8,128)} %get-tuple-element.12, f32[12,2,16,64]{3,2,1,0:T(8,128)} %get-tuple-element.11), kind=kLoop, calls=%fused_computation.1 | loop fusion | bytes 294912 | tf_op jit(solution)/shard_map/transpose | solution.py:435
  24.4 0.7 %reshape.25 = f32[2,9216]{1,0:T(2,128)} reshape(f32[2,12,12,64]{3,2,1,0:T(8,128)S(1)} %copy.13) | data formatting | bytes 147456 | tf_op jit(solution)/shard_map/reshape | solution.py:435
  25.2 0.7 %reshape.24 = f32[2,9216]{1,0:T(2,128)} reshape(f32[2,12,12,64]{3,2,1,0:T(8,128)S(1)} %copy.12) | data formatting | bytes 147456 | tf_op jit(solution)/shard_map/reshape | solution.py:435
  25.9 24.2 %gather_slots.1.refs_1_ = bf16[16,12,16,256]{3,2,1,0:T(8,128)(2,1)} custom-call(bf16[2,12,16,256]{3,2,1,0:T(8,128)(2,1)} %get-tuple-element.8.pay_ref.refs_0_), custom_call_target="tpu_custom_call" | custom-call | flops 1 | bytes 8388608 | tf_op jit(solution)/shard_map/gather_slots/pallas_call | solution.py:380
  50.1 21.0 %dictionary.1 = bf16[7744,256]{1,0:T(8,128)(2,1)} custom-call(bf16[7744,256]{1,0:T(8,128)(2,1)} %bitcast.18, bf16[16,12,16,256]{3,2,1,0:T(8,128)(2,1)} %gather_slots.1.refs_1_), custom_call_target="tpu_custom_call" | custom-call | flops 9135194112 | bytes 8388608 | tf_op jit(solution)/shard_map/dictionary/pallas_call | solution.py:414
  (5 shorter events, 0.1 us)

commit v4 on v3

--- a/solution.py
+++ b/solution.py
@@ -173,7 +173,7 @@
         pay_ref[s] = stage[:, s, :, :].astype(BF16)
 
 
-def second_kernel(f_ref, pay_ref, codes_ref, duals_ref, codes_out, duals_out, rpad, ftail, zpad):
+def second_codes(f_ref, pay_ref, codes_ref, duals_ref, codes_out, duals_out, rpad, ftail, zpad):
     slots = pay_ref.shape[0]
     rpad[...] = jnp.zeros_like(rpad)
     zpad[...] = jnp.zeros_like(zpad)
@@ -195,7 +195,8 @@
 
 
 def gather_kernel(
-    outer, inner, pay_ref, all_ref, other, pair_send, pair_recv, z_send, z_recv,
+    outer, inner, f_ref, pay_ref, codes_ref, duals_ref, all_ref, codes_out, duals_out,
+    rpad, ftail, zpad, other, pair_send, pair_recv, z_send, z_recv,
     y_send, y_recv, c_send, c_recv
 ):
     me = lax.axis_index("tile")
@@ -254,6 +255,7 @@
     for dy in range(1, inner):
         start(along_y(0, dy))
     start(across(0, 0))
+    second_codes(f_ref, pay_ref, codes_ref, duals_ref, codes_out, duals_out, rpad, ftail, zpad)
     for dz in range(1, outer):
         arrived(all_ref.at[index(-dz, 0, core)], z_recv.at[dz], z_send.at[dz])
         for dy in range(1, inner):
@@ -270,8 +272,9 @@
         one.wait_send()
 
 
-def dictionary_kernel(stride, f_ref, all_ref, new_ref, maps, taps, stage, total):
+def dictionary_kernel(stride, steps, f_hbm, all_ref, new_hbm, maps, taps, stage, total, f_ref, new_ref, f_sem, new_sem):
     at = pl.program_id(0)
+    fetch = pltpu.make_async_copy(f_hbm, f_ref, f_sem)
     group = all_ref.shape[0]
     row = group * JP
     rows = SIDE * row
@@ -279,9 +282,11 @@
 
     @pl.when(at == 0)
     def _():
+        fetch.start()
         maps[...] = jnp.zeros_like(maps)
         taps[...] = jnp.zeros_like(taps)
-        total[...] = jnp.zeros_like(total)
+        if steps > 1:
+            total[...] = jnp.zeros_like(total)
 
     for d in range(group):
         stage[:, d, :, :] = all_ref[d].astype(F32)
@@ -300,29 +305,55 @@
     values = stage[...]
     place = lax.broadcasted_iota(jnp.int32, values.shape, 2)
     residual = jnp.where(place < SIDE, values, 0.0).reshape(rows, C).astype(BF16)
-    for a in range(K):
-        total[a * LAST : (a + 1) * LAST, :] += jnp.dot(
+    @pl.when(at == 0)
+    def _():
+        fetch.wait()
+
+    def term(a):
+        return jnp.dot(
             taps[:, a * row : a * row + rows], residual, preferred_element_type=F32
         )
 
-    @pl.when(at == pl.num_programs(0) - 1)
-    def _():
-        def step(t, squares):
-            part = pl.ds(pl.multiple_of(t * M, M), M)
-            moved = f_ref[part, :].astype(F32) - (stride * FACTOR) * total[part, :]
-            total[part, :] = moved
-            return squares + moved * moved
-
-        squares = lax.fori_loop(0, K * K, step, jnp.zeros((M, C), F32), unroll=11)
+    def finish(part, summed):
+        return f_ref[part, :].astype(F32) - (stride * FACTOR) * summed
+
+    def close(squares):
         sums = jnp.sum(squares, axis=1, keepdims=True)
         inverse = 1.0 / jnp.sqrt(sums / (C * K * K) + EPSILON)
-
-        def scale(t, carry):
-            part = pl.ds(pl.multiple_of(t * M, M), M)
-            new_ref[part, :] = (total[part, :] * inverse).astype(BF16)
-            return carry
-
-        lax.fori_loop(0, K * K, scale, 0, unroll=11)
+        inverse = jnp.broadcast_to(inverse, (M, C))
+        sends = []
+        for a in range(K):
+            part = slice(a * LAST, (a + 1) * LAST)
+            values = total[part, :].reshape(K, M, C) * inverse[None]
+            new_ref[part, :] = values.reshape(LAST, C).astype(BF16)
+            send = pltpu.make_async_copy(new_ref.at[part], new_hbm.at[part], new_sem.at[a])
+            send.start()
+            sends.append(send)
+        for send in sends:
+            send.wait()
+
+    if steps == 1:
+        squares = jnp.zeros((M, C), F32)
+        for a in range(K):
+            part = slice(a * LAST, (a + 1) * LAST)
+            moved = finish(part, term(a))
+            total[part, :] = moved
+            squares = squares + jnp.sum((moved * moved).reshape(K, M, C), axis=0)
+        close(squares)
+        return
+
+    for a in range(K):
+        total[a * LAST : (a + 1) * LAST, :] += term(a)
+
+    @pl.when(at == steps - 1)
+    def _():
+        squares = jnp.zeros((M, C), F32)
+        for a in range(K):
+            part = slice(a * LAST, (a + 1) * LAST)
+            moved = finish(part, total[part, :])
+            total[part, :] = moved
+            squares = squares + jnp.sum((moved * moved).reshape(K, M, C), axis=0)
+        close(squares)
 
 
 def in_vmem():
@@ -377,12 +408,13 @@
     inner = 1 << ((chips.bit_length() - 1) // 2)
     outer = chips // inner
     dma = pltpu.SemaphoreType.DMA
-    everyone = pl.pallas_call(
+    everyone, codes, duals = pl.pallas_call(
         lambda *refs: gather_kernel(outer, inner, *refs),
-        out_shape=jax.ShapeDtypeStruct((groups, SIDE, JP, C), BF16),
-        in_specs=[in_vmem()],
-        out_specs=in_vmem(),
-        scratch_shapes=[
+        out_shape=(jax.ShapeDtypeStruct((groups, SIDE, JP, C), BF16), state, state),
+        in_specs=[in_vmem()] * 4,
+        out_specs=(in_vmem(),) * 3,
+        scratch_shapes=back
+        + [
             pltpu.VMEM((SIDE, JP, C), BF16),
             dma,
             dma,
@@ -396,35 +428,30 @@
         compiler_params=pltpu.CompilerParams(
             vmem_limit_bytes=LIMIT, collective_id=0, has_side_effects=True
         ),
-        cost_estimate=cost(1),
+        cost_estimate=cost(one_product),
         name="gather_slots",
-    )(payload)
-    codes, duals = pl.pallas_call(
-        second_kernel,
-        out_shape=(state, state),
-        in_specs=[in_vmem()] * 4,
-        out_specs=(in_vmem(),) * 2,
-        scratch_shapes=back,
-        compiler_params=pltpu.CompilerParams(vmem_limit_bytes=LIMIT),
-        cost_estimate=cost(one_product),
-        name="second_codes",
     )(filters.T, payload, codes_mid, duals_mid)
-    group = 8
+    group = 16 if groups % 16 == 0 else 8
+    steps = groups // group
     columns = filters.T
     new_filters = pl.pallas_call(
-        lambda *refs: dictionary_kernel(stride, *refs),
-        grid=(groups // group,),
+        lambda *refs: dictionary_kernel(stride, steps, *refs),
+        grid=(steps,),
         out_shape=jax.ShapeDtypeStruct((COLS, C), BF16),
         in_specs=[
-            pl.BlockSpec((COLS, C), lambda g: (0, 0), pipeline_mode=pl.Buffered(1)),
+            pl.BlockSpec(memory_space=pl.ANY),
             pl.BlockSpec((group, SIDE, JP, C), lambda g: (g, 0, 0, 0)),
         ],
-        out_specs=pl.BlockSpec((COLS, C), lambda g: (0, 0), pipeline_mode=pl.Buffered(1)),
+        out_specs=pl.BlockSpec(memory_space=pl.ANY),
         scratch_shapes=[
             pltpu.VMEM((SIDE, group, JP, M), F32),
             pltpu.VMEM((LAST, 22 * group * JP), BF16),
             pltpu.VMEM((SIDE, group, JP, C), F32),
             pltpu.VMEM((COLS, C), F32),
+            pltpu.VMEM((COLS, C), BF16),
+            pltpu.VMEM((COLS, C), BF16),
+            dma,
+            dma((K,)),
         ],
         compiler_params=pltpu.CompilerParams(vmem_limit_bytes=LIMIT),
         cost_estimate=cost(groups * one_product // 2),

time: 71.4 us -> 65.8 us (0.922)
  Pallas kernels: 63 us -> 57.2 us
    pallas_call x2 -> x1, Pallas kernels: 26.2 us -> 18.9 us  [local(): pl.pallas_call(lambda *refs: dictionary_kernel(stride, steps, *refs), gri...]
    pallas_call x1, Pallas kernels: 24.2 us -> 25.7 us  [local(): pl.pallas_call(lambda *refs: gather_kernel(outer, inner, *refs), out_shap...]
where the time goes in v4:
time: 65.8 us; the launch traced here: 65.4 us
  Pallas kernels  57.2 us (87%)
  local copies, waits for them, and re-layouts  7.42 us (11%)
  between operations  0.85 us (1%)
    pallas_call x1, Pallas kernels, local(): pl.pallas_call(lambda *refs: gather_kernel(outer, inner, *refs), out_shap...  25.7 us
    pallas_call x1, Pallas kernels, local(): pl.pallas_call(lambda *refs: dictionary_kernel(stride, steps, *refs), gri...  18.9 us
    pallas_call x1, Pallas kernels, local(): pl.pallas_call(first_kernel, out_shape=(jax.ShapeDtypeStruct((slots, SIDE...  12.6 us
    pad x3, local copies, waits for them, and re-layouts, arranged(): return jnp.pad(shaped, ((0, 0), (0, 0), (0, JP - SIDE), (0, 0)))  2.01 us
    reshape x5, local copies, waits for them, and re-layouts, arranged(): shaped = array.reshape(slots, SIDE, SIDE, width).transpose(1, 0, 2, 3)  1.81 us
    reshape x2, local copies, waits for them, and re-layouts, flat(): array[:, :, 0:SIDE, :].transpose(1, 0, 2, 3).reshape(slots, SIDE * SIDE * M)  1.49 us

profile of v4, /device:TPU:0, one launch (start us, length us, event | category | flops | bytes accessed | tf_op | source)
XLA Modules:
  0.0 65.4 jit_solution(9899850318626031547)
XLA Ops:
  0.6 0.9 %reshape.22 = bf16[2,12,12,64]{3,2,1,0:T(8,128)(2,1)S(1)} reshape(bf16[2,9216]{1,0:T(2,128)(2,1)} %param.8) | data formatting | bytes 73728 | tf_op jit(solution)/shard_map/reshape | solution.py:376
  1.5 0.7 %pad.12.codes_ref = bf16[12,2,16,64]{3,2,1,0:T(8,128)(2,1)} pad(bf16[12,2,12,64]{3,2,1,0:T(8,128)(2,1)S(1)} %bitcast.21, bf16[]{:T(256)} %constant.2.clone.1), padding=0_0x0_0x0_4x0_0 | pad | bytes 86018 | tf_op jit(solution)/shard_map/jit(_pad)/pad | solution.py:377
  2.2 0.9 %reshape.23 = bf16[2,12,12,64]{3,2,1,0:T(8,128)(2,1)S(1)} reshape(bf16[2,9216]{1,0:T(2,128)(2,1)} %param.9) | data formatting | bytes 73728 | tf_op jit(solution)/shard_map/reshape | solution.py:376
  3.1 0.7 %pad.13.duals_ref = bf16[12,2,16,64]{3,2,1,0:T(8,128)(2,1)} pad(bf16[12,2,12,64]{3,2,1,0:T(8,128)(2,1)S(1)} %bitcast.22, bf16[]{:T(256)} %constant.2.clone.1), padding=0_0x0_0x0_4x0_0 | pad | bytes 86018 | tf_op jit(solution)/shard_map/jit(_pad)/pad | solution.py:377
  3.8 1.0 %copy.8 = bf16[2,144,256]{2,0,1:T(2,128)(2,1)S(1)} copy(bf16[2,144,256]{2,1,0:T(8,128)(2,1)} %param.5) | data formatting | bytes 294912 | tf_op args[0]
  4.8 0.7 %pad.11.img_ref = bf16[12,2,16,256]{3,2,1,0:T(8,128)(2,1)} pad(bf16[12,2,12,256]{3,2,1,0:T(8,128)(2,1)S(1)} %bitcast.19, bf16[]{:T(256)} %constant.2.clone.1), padding=0_0x0_0x0_4x0_0 | pad | bytes 344066 | tf_op jit(solution)/shard_map/jit(_pad)/pad | solution.py:377
  5.5 12.6 %first_pass.1 = (bf16[2,12,16,256]{3,2,1,0:T(8,128)(2,1)}, f32[12,2,16,64]{3,2,1,0:T(8,128)}, f32[12,2,16,64]{3,2,1,0:T(8,128)}) custom-call(s32[2]{0:T(128)} %rows_ref.1, bf16[7744,256]{1,0:T(8,128)(2,1)} %bitcast.16, bf16[12,2,16,256]{3,2,1,0:T(8,128)(2,1)} %pad.11.img_ref, bf16[12,2,16,64]{3,2,1,0:T(8,128)(2,1)} %pad.12.codes_ref, ...), custom_call_target="tpu_custom_call" | custom-call | flops 3425697792 | bytes 8388608 | tf_op jit(solution)/shard_map/first_pass/pallas_call | solution.py:386
  18.1 25.7 %gather_slots.1 = (bf16[16,12,16,256]{3,2,1,0:T(8,128)(2,1)}, f32[12,2,16,64]{3,2,1,0:T(8,128)}, f32[12,2,16,64]{3,2,1,0:T(8,128)}) custom-call(bf16[7744,256]{1,0:T(8,128)(2,1)} %bitcast.17, bf16[2,12,16,256]{3,2,1,0:T(8,128)(2,1)} %get-tuple-element.9.refs_1_, f32[12,2,16,64]{3,2,1,0:T(8,128)} %get-tuple-element.10.refs_2_, ...), custom_call_target="tpu_custom_call" | custom-call | flops 1141899264 | bytes 8388608 | tf_op jit(solution)/shard_map/gather_slots/pallas_call | solution.py:411
  43.8 1.0 %slice_bitcast_fusion = (f32[2,12,12,64]{3,2,0,1:T(8,128)S(1)}, f32[2,12,12,64]{3,2,0,1:T(8,128)S(1)}) fusion(f32[12,2,16,64]{3,2,1,0:T(8,128)} %get-tuple-element.13, f32[12,2,16,64]{3,2,1,0:T(8,128)} %get-tuple-element.12), kind=kLoop, calls=%fused_computation.1 | loop fusion | bytes 294912 | tf_op jit(solution)/shard_map/transpose | solution.py:462
  44.8 0.7 %reshape.25 = f32[2,9216]{1,0:T(2,128)} reshape(f32[2,12,12,64]{3,2,1,0:T(8,128)S(1)} %copy.13) | data formatting | bytes 147456 | tf_op jit(solution)/shard_map/reshape | solution.py:462
  45.6 0.7 %reshape.24 = f32[2,9216]{1,0:T(2,128)} reshape(f32[2,12,12,64]{3,2,1,0:T(8,128)S(1)} %copy.12) | data formatting | bytes 147456 | tf_op jit(solution)/shard_map/reshape | solution.py:462
  46.4 18.9 %dictionary.1 = bf16[7744,256]{1,0:T(8,128)(2,1)} custom-call(bf16[7744,256]{1,0:T(8,128)(2,1)} %bitcast.18, bf16[16,12,16,256]{3,2,1,0:T(8,128)(2,1)} %get-tuple-element.14.refs_1_), custom_call_target="tpu_custom_call" | custom-call | flops 9135194112 | bytes 8388608 | tf_op jit(solution)/shard_map/dictionary/pallas_call | solution.py:437
  (5 shorter events, 0.1 us)
